TPU v7x, 32 devices: a whole 2x2x4 slice. The times are simulated.
32 devices in a mesh: wide: 8 (over y, x, core), narrow: 4 (over z).
Axes of the slice: x: 2, y: 2, z: 4, core: 2. Of those that a mesh axis runs over, the one named last changes fastest.
Arguments:
- amplitudes: float32 [2, 8, 4, 16, 256, 256], P(None, 'wide', 'narrow'), may hold values from -6 to 6
- low_gate: float32 [2, 256, 256], replicated, may hold values from -0.25 to 0.25
- mid_gate: float32 [2, 256, 256], replicated, may hold values from -0.25 to 0.25
- pair_gates: float32 [3, 2, 4, 4], replicated, may hold values from -2 to 2
Outputs:
- remapped: float32 [2, 8, 4, 16, 256, 256], P(None, 'wide', 'narrow')
All inputs are finite; a program needn't handle non-finite values.
Results may differ from a plain program's by a relative error of at most 0.00007.
Values sent between devices are 32-bit elements; how exact they have to be, the bound alone decides.
A program may use at most 128 MiB of HBM per device.

v0:
```python
import jax
import jax.numpy as jnp
from jax import lax
from jax.sharding import PartitionSpec as P

highest = lax.Precision.HIGHEST


def swapped(x, axis, bit):
    return lax.ppermute(x, axis, [(i, i ^ 1 << bit) for i in range(lax.axis_size(axis))])


def apply_merged(amplitudes, low_gate, mid_gate):
    real_part, imag_part = (amplitudes[0], amplitudes[1])
    low_real, low_imag = (low_gate[0], low_gate[1])
    first_real = jnp.einsum("abhml,il->abhmi", real_part, low_real, precision=highest) - jnp.einsum(
        "abhml,il->abhmi", imag_part, low_imag, precision=highest
    )
    first_imag = jnp.einsum("abhml,il->abhmi", real_part, low_imag, precision=highest) + jnp.einsum(
        "abhml,il->abhmi", imag_part, low_real, precision=highest
    )
    mid_real, mid_imag = (mid_gate[0], mid_gate[1])
    second_real = jnp.einsum(
        "abhml,im->abhil", first_real, mid_real, precision=highest
    ) - jnp.einsum("abhml,im->abhil", first_imag, mid_imag, precision=highest)
    second_imag = jnp.einsum(
        "abhml,im->abhil", first_real, mid_imag, precision=highest
    ) + jnp.einsum("abhml,im->abhil", first_imag, mid_real, precision=highest)
    return jnp.stack([second_real, second_imag])


def partner_gate(state, other, gate, mine, half_bit):
    rows = lax.dynamic_slice_in_dim(gate, 2 * mine, 2, 1)
    own_cols = lax.dynamic_slice_in_dim(rows, 2 * mine, 2, 2)
    far_cols = lax.dynamic_slice_in_dim(rows, 2 - 2 * mine, 2, 2)
    shape = state.shape
    split_shape = shape[:3] + (shape[3] >> half_bit + 1, 2, 1 << half_bit) + shape[4:]
    own_split = state.reshape(split_shape)
    far_split = other.reshape(split_shape)
    outputs = []
    for target in range(2):
        total_real = jnp.zeros(own_split[0, :, :, :, 0].shape, jnp.float32)
        total_imag = jnp.zeros(own_split[0, :, :, :, 0].shape, jnp.float32)
        for source in range(2):
            for coeffs, piece in ((own_cols, own_split), (far_cols, far_split)):
                amplitude = piece[:, :, :, :, source]
                coef_real = coeffs[0, target, source]
                coef_imag = coeffs[1, target, source]
                total_real = total_real + coef_real * amplitude[0] - coef_imag * amplitude[1]
                total_imag = total_imag + coef_real * amplitude[1] + coef_imag * amplitude[0]
        outputs.append(jnp.stack([total_real, total_imag]))
    return jnp.stack(outputs, axis=4).reshape(shape)


def narrow_gate(state, gate):
    other = swapped(state, "narrow", 1)
    mine = lax.axis_index("narrow") >> 1 & 1
    return partner_gate(state, other, gate, mine, 0)


def remap_qubits(state):
    return lax.all_to_all(state, "wide", split_axis=4, concat_axis=4, tiled=True)


def body(amplitudes, low_gate, mid_gate, pair_gates):
    state = apply_merged(amplitudes, low_gate, mid_gate)
    wide_index = lax.axis_index("wide")
    other = swapped(state, "wide", 0)
    state = partner_gate(state, other, pair_gates[0], wide_index & 1, 0)
    other = swapped(state, "wide", 2)
    state = partner_gate(state, other, pair_gates[1], wide_index >> 2 & 1, 1)
    state = narrow_gate(state, pair_gates[2])
    state = remap_qubits(state)
    return state


def solution(mesh):
    in_specs = (P(None, "wide", "narrow", None, None, None), P(), P(), P())
    out_specs = P(None, "wide", "narrow", None, None, None)
    return jax.shard_map(body, mesh=mesh, in_specs=in_specs, out_specs=out_specs, check_vma=False)
```

profile of v0, /device:TPU:0, one launch (start us, length us, event | category | flops | bytes accessed | tf_op | source)
XLA Modules:
  0.0 852.5 jit_solution(16217510723273503916)
XLA Ops:
  0.0 5.5 fusion.2
  5.5 0.0 copy-start.10
  5.5 4.5 fusion
  10.0 3.5 fusion.12
  13.5 6.9 fusion.42
  20.4 7.0 fusion.46
  27.3 3.7 fusion.15
  31.0 7.1 convolution_add_fusion
  38.1 7.5 convolution_subtract_fusion
  45.6 4.3 pad_maximum_fusion
  49.9 0.2 copy-done
  50.1 0.4 collective-permute-start
  50.6 4.6 fusion.62
  55.2 1.9 copy.186
  57.1 4.6 fusion.63
  61.7 2.9 copy.185
  64.6 2.9 copy.182
  67.5 2.9 copy.181
  70.4 0.1 dynamic-slice_bitcast_fusion.3
  70.5 0.7 fusion.70
  71.2 0.7 fusion.69
  71.8 6.9 fusion.61
  78.8 2.9 copy.188
  81.7 2.9 copy.187
  84.5 2.9 copy.184
  87.5 2.9 copy.183
  90.3 11.9 %add_subtract_fusion = (f32[1,1,1,8,1,1,256,256]{7,6,3,5,4,2,1,0:T(8,128)S(1)}, f32[1,1,1,8,1,1,256,256]{7,6,3,5,4,2,1,0:T(8,128)S(1)}) fusion(f32[1,1,1,8,1,1,256,256]{7,6,3,5,4,2,1,0:T(8,128)} %copy.188, f32[1,1,1,8,1,1,256,256]{7,6,3,5,4,2,1,0:T(8,128)} %copy.187, f32[1,1,1,8,1,1,256,256]{7,6,3,5,4,2,1,0:T(8,128)S(1)} %copy.186, ...), kind=kLoop, calls=%fused_computation.74 | loop fusion | flops 15728640 | bytes 20971552 | tf_op jit(solution)/shard_map/sub | solution.py:49
  102.3 0.4 maximum_bitcast_fusion.1
  102.8 1.1 copy-done.3
  103.9 0.6 copy-done.4
  104.5 0.6 copy-done.5
  105.1 0.6 copy-done.6
  105.7 6.9 add_subtract_fusion.1
  112.7 0.4 maximum_bitcast_fusion
  113.1 4.0 pad_maximum_fusion.1
  117.0 2.5 collective-permute-start.1
  119.5 0.6 fusion.68
  120.2 0.7 fusion.67
  120.8 3.6 maximum_maximum_fusion
  124.5 4.0 fusion.60
  128.5 172.4 %collective-permute-done.1 = f32[2,1,1,16,256,256]{5,4,3,0,2,1:T(8,128)S(1)} collective-permute-done((f32[2,1,1,16,256,256]{5,4,3,0,2,1:T(8,128)}, f32[2,1,1,16,256,256]{5,4,3,0,2,1:T(8,128)S(1)}, u32[]{:S(2)}, u32[]{:S(2)}) %collective-permute-start.1) | collective-permute-done | bytes 8388640 | tf_op jit(solution)/shard_map/ppermute | solution.py:10
  300.9 6.0 fusion.33
  306.9 6.0 fusion.41
  312.8 6.1 fusion.39
  318.9 6.2 fusion.36
  325.2 0.3 maximum_bitcast_fusion.3
  325.5 0.3 maximum_bitcast_fusion.2
  325.8 0.9 pad_maximum_fusion.2
  326.6 4.0 copy.153
  330.6 2.8 collective-permute-start.2
  333.4 0.1 dynamic-slice_bitcast_fusion.5
  333.5 0.7 fusion.65
  334.1 359.7 %collective-permute-done.2 = f32[2,1,1,16,256,256]{5,4,3,0,2,1:T(8,128)} collective-permute-done((f32[2,1,1,16,256,256]{5,4,3,0,2,1:T(8,128)}, f32[2,1,1,16,256,256]{5,4,3,0,2,1:T(8,128)}, u32[]{:S(2)}, u32[]{:S(2)}) %collective-permute-start.2) | collective-permute-done | bytes 8388640 | tf_op jit(solution)/shard_map/ppermute | solution.py:10
  693.9 11.3 %fusion.18 = f32[1,1,1,8,1,256,256]{6,5,3,4,2,1,0:T(8,128)S(1)} fusion(f32[2,1,1,8,2,1,256,256]{7,6,4,3,0,5,2,1:T(8,128)} %bitcast.92, f32[2,1,1,8,2,1,256,256]{7,6,4,3,0,5,2,1:T(8,128)} %bitcast.97, f32[]{:T(128)} %bitcast.117, f32[]{:T(128)} %bitcast.116, f32[]{:T(128)} %bitcast.114, f32[]{:T(128)} %bitcast.113, f32[]{:T(128)} %bitcast.112, f32[]{:T(128)} %bitcast.111, ...), kind=kLoop, calls=%fused_computation.38 | loop fusion | flops 7864320 | bytes 18874400 | tf_op jit(solution)/shard_map/add | solution.py:50
  705.2 11.3 %fusion.32 = f32[1,1,1,8,1,256,256]{6,5,3,4,2,1,0:T(8,128)S(1)} fusion(f32[2,1,1,8,2,1,256,256]{7,6,4,3,0,5,2,1:T(8,128)} %bitcast.92, f32[2,1,1,8,2,1,256,256]{7,6,4,3,0,5,2,1:T(8,128)} %bitcast.97, f32[]{:T(128)} %bitcast.117, f32[]{:T(128)} %bitcast.116, f32[]{:T(128)} %bitcast.114, f32[]{:T(128)} %bitcast.113, f32[]{:T(128)} %bitcast.112, f32[]{:T(128)} %bitcast.111, ...), kind=kLoop, calls=%fused_computation.58 | loop fusion | flops 7864320 | bytes 18874400 | tf_op jit(solution)/shard_map/sub | solution.py:49
  716.5 11.3 %fusion.28 = f32[1,1,1,8,1,256,256]{6,5,3,0,4,2,1:T(8,128)S(1)} fusion(f32[2,1,1,8,2,1,256,256]{7,6,4,3,0,5,2,1:T(8,128)} %bitcast.92, f32[2,1,1,8,2,1,256,256]{7,6,4,3,0,5,2,1:T(8,128)} %bitcast.97, f32[]{:T(128)} %bitcast.103, f32[]{:T(128)} %bitcast.102, f32[]{:T(128)} %bitcast.100, f32[]{:T(128)} %bitcast.99, f32[]{:T(128)} %bitcast.98, f32[]{:T(128)} %bitcast.95, ...), kind=kLoop, calls=%fused_computation.54 | loop fusion | flops 7864320 | bytes 18874400 | tf_op jit(solution)/shard_map/add | solution.py:50
  727.8 11.3 %fusion.23 = f32[1,1,1,8,1,256,256]{6,5,3,0,4,2,1:T(8,128)S(1)} fusion(f32[2,1,1,8,2,1,256,256]{7,6,4,3,0,5,2,1:T(8,128)} %bitcast.92, f32[2,1,1,8,2,1,256,256]{7,6,4,3,0,5,2,1:T(8,128)} %bitcast.97, f32[]{:T(128)} %bitcast.103, f32[]{:T(128)} %bitcast.102, f32[]{:T(128)} %bitcast.100, f32[]{:T(128)} %bitcast.99, f32[]{:T(128)} %bitcast.98, f32[]{:T(128)} %bitcast.95, ...), kind=kLoop, calls=%fused_computation.49 | loop fusion | flops 7864320 | bytes 18874400 | tf_op jit(solution)/shard_map/sub | solution.py:49
  739.1 0.3 maximum_bitcast_fusion.5
  739.4 0.3 maximum_bitcast_fusion.4
  739.7 0.9 pad_maximum_fusion.3
  740.6 0.9 copy.171
  741.4 4.9 copy.172
  746.3 97.8 %all_to_all.5 = f32[2,1,1,16,256,256]{5,3,0,2,1,4:T(8,128)S(1)} all-to-all(f32[2,1,1,16,256,256]{5,3,0,2,1,4:T(8,128)S(1)} %copy.172), channel_id=1, replica_groups=mesh['wide'=8,'narrow'=4] {'wide'}, dimensions={4} | all-to-all | bytes 16777216 | tf_op jit(solution)/shard_map/all_to_all | solution.py:62
  844.1 8.3 copy.173
  (22 shorter events, 0.0 us)
Async XLA Ops:
  0.0 5.5 copy-start.2
  5.5 4.5 copy-start.10
  10.0 3.5 copy-start.11
  38.1 7.5 copy-start.1
  45.6 4.5 copy-start
  50.1 21.7 %collective-permute-start = (f32[2,1,1,16,256,256]{4,5,3,2,1,0:T(8,128)}, f32[2,1,1,16,256,256]{4,5,3,2,1,0:T(8,128)}, u32[]{:S(2)}, u32[]{:S(2)}) collective-permute-start(f32[2,1,1,16,256,256]{4,5,3,2,1,0:T(8,128)} %pad_maximum_fusion), channel_id=1, source_target_pairs={{0,4},{4,0},{8,12},{12,8},{16,20},{20,16},{24,28},{28,24},{1,5},{5... | collective-permute-start | bytes 25165832 | tf_op jit(solution)/shard_map/ppermute | solution.py:10
  67.5 2.9 copy-start.12
  90.3 12.4 %copy-start.7 = (f32[1,1,1,8,1,1,256,256]{7,6,3,5,4,2,1,0:T(8,128)S(1)}, f32[1,1,1,8,1,1,256,256]{7,6,3,5,4,2,1,0:T(8,128)}, u32[]{:S(2)}) copy-start(f32[1,1,1,8,1,1,256,256]{7,6,3,5,4,2,1,0:T(8,128)} %copy.187) | copy-start | bytes 6291460
  90.3 12.4 %copy-start.8 = (f32[1,1,1,8,1,1,256,256]{7,6,3,5,4,2,1,0:T(8,128)S(1)}, f32[1,1,1,8,1,1,256,256]{7,6,3,5,4,2,1,0:T(8,128)}, u32[]{:S(2)}) copy-start(f32[1,1,1,8,1,1,256,256]{7,6,3,5,4,2,1,0:T(8,128)} %copy.184) | copy-start | bytes 6291460
  90.3 12.4 %copy-start.9 = (f32[1,1,1,8,1,1,256,256]{7,6,3,5,4,2,1,0:T(8,128)S(1)}, f32[1,1,1,8,1,1,256,256]{7,6,3,5,4,2,1,0:T(8,128)}, u32[]{:S(2)}) copy-start(f32[1,1,1,8,1,1,256,256]{7,6,3,5,4,2,1,0:T(8,128)} %copy.183) | copy-start | bytes 6291460
  102.3 1.6 copy-start.3
  102.3 2.2 copy-start.4
  102.3 2.8 copy-start.5
  102.3 3.4 copy-start.6
  117.0 183.9 %collective-permute-start.1 = (f32[2,1,1,16,256,256]{5,4,3,0,2,1:T(8,128)}, f32[2,1,1,16,256,256]{5,4,3,0,2,1:T(8,128)S(1)}, u32[]{:S(2)}, u32[]{:S(2)}) collective-permute-start(f32[2,1,1,16,256,256]{5,4,3,0,2,1:T(8,128)} %bitcast.372), channel_id=1, source_target_pairs={{0,16},{4,20},{8,24},{12,28},{16,0},{20,4},{24,8},{28,12},{1,17},{... | collective-permute-start | bytes 25165832 | tf_op jit(solution)/shard_map/ppermute | solution.py:10
  330.6 363.3 %collective-permute-start.2 = (f32[2,1,1,16,256,256]{5,4,3,0,2,1:T(8,128)}, f32[2,1,1,16,256,256]{5,4,3,0,2,1:T(8,128)}, u32[]{:S(2)}, u32[]{:S(2)}) collective-permute-start(f32[2,1,1,16,256,256]{5,4,3,0,2,1:T(8,128)} %bitcast.96), channel_id=1, source_target_pairs={{0,2},{1,3},{2,0},{3,1},{4,6},{5,7},{6,4},{7,5},{8,10},{9,11},{10,... | collective-permute-start | bytes 25165832 | tf_op jit(solution)/shard_map/ppermute | solution.py:10
where the time goes:
time: 863 us; the launch traced here: 853 us
  waiting for transfers between devices  532 us (62%)
  other arithmetic  104 us (12%)
  blocking collectives  97.8 us (11%)
  local copies, waits for them, and re-layouts  66.9 us (8%)
  matrix products  45.5 us (5%)
    ppermute x3, waiting for transfers between devices, swapped(): lax.ppermute(x, axis, [(i, i ^ 1 << bit) for i in range(lax.axis_size(axi...  532 us
    all_to_all x1, blocking collectives, remap_qubits(): lax.all_to_all(state, 'wide', split_axis=4, concat_axis=4, tiled=True)  97.8 us
    sub x6, other arithmetic, partner_gate(): total_real + coef_real * amplitude[0] - coef_imag * amplitude[1]  53.6 us
    add x4, other arithmetic, partner_gate(): total_imag + coef_real * amplitude[1] + coef_imag * amplitude[0]  34.7 us
    unnamed x34, local copies, waits for them, and re-layouts  25.4 us
  transfers between devices with their start and end apart: 3, of which 2 were waited for; matrix products, arithmetic and copies ran while one was open for 4% of the time, Pallas kernels for 0%

commit v1 on v0

v1 whole, which is shorter than its diff:
```python
import functools

import jax
import jax.numpy as jnp
from jax import lax
from jax.experimental import pallas as pl
from jax.experimental.pallas import tpu as pltpu
from jax.sharding import PartitionSpec as P

MESH = pl.DeviceIdType.MESH
CHUNK = 8
highest = lax.Precision.HIGHEST


def merged(x, slot, low, mid):
    gate, lanes = x.shape[2], x.shape[3]
    both = x[slot].reshape(2 * gate, lanes)
    dims = (((1,), (1,)), ((), ()))
    by_real = lax.dot_general(both, low[0], dims, precision=highest, preferred_element_type=jnp.float32)
    by_imag = lax.dot_general(both, low[1], dims, precision=highest, preferred_element_type=jnp.float32)
    first_real = by_real[:gate] - by_imag[gate:]
    first_imag = by_imag[:gate] + by_real[gate:]
    mid_both = mid[...].reshape(2 * gate, gate)
    on_real = jnp.dot(mid_both, first_real, precision=highest, preferred_element_type=jnp.float32)
    on_imag = jnp.dot(mid_both, first_imag, precision=highest, preferred_element_type=jnp.float32)
    x[slot, 0] = on_real[:gate] - on_imag[gate:]
    x[slot, 1] = on_real[gate:] + on_imag[:gate]


def mix(coefs, sources):
    real, imag = None, None
    for (coef_real, coef_imag), (in_real, in_imag) in zip(coefs, sources):
        term_real = coef_real * in_real - coef_imag * in_imag
        term_imag = coef_real * in_imag + coef_imag * in_real
        real = term_real if real is None else real + term_real
        imag = term_imag if imag is None else imag + term_imag
    return real, imag


def pair_on(ref, slots, stride, gates, which):
    coefs = [
        [(gates[which * 32 + row * 4 + col], gates[which * 32 + 16 + row * 4 + col]) for col in range(4)]
        for row in range(4)
    ]
    per = stride // CHUNK

    def step(i, _):
        base = pl.multiple_of((i // per) * (2 * stride) + (i % per) * CHUNK, CHUNK)
        far = pl.multiple_of(base + stride, CHUNK)
        places = [(slots[b], pl.ds(start, CHUNK)) for start in (base, far) for b in range(2)]
        sources = [(ref[s, 0, rows], ref[s, 1, rows]) for s, rows in places]
        results = [mix(coefs[row], sources) for row in range(4)]
        for (s, rows), (real, imag) in zip(places, results):
            ref[s, 0, rows] = real
            ref[s, 1, rows] = imag
        return 0

    lax.fori_loop(0, ref.shape[2] // (2 * CHUNK), step, 0)


def combine(own, far, slots, side, gates):
    def coef(q, a, b):
        at = 64 + (2 * side + q) * 4 + 2 * a + b
        return gates[at], gates[at + 16]

    coefs = [[coef(q, side, 0), coef(q, side, 1), coef(q, 1 - side, 0), coef(q, 1 - side, 1)] for q in range(2)]

    def step(i, _):
        rows = pl.ds(pl.multiple_of(i * CHUNK, CHUNK), CHUNK)
        sources = [(ref[s, 0, rows], ref[s, 1, rows]) for ref in (own, far) for s in slots]
        results = [mix(coefs[q], sources) for q in range(2)]
        for s, (real, imag) in zip(slots, results):
            far[s, 0, rows] = real
            far[s, 1, rows] = imag
        return 0

    lax.fori_loop(0, far.shape[2] // CHUNK, step, 0)


def kernel(n_wide, psi, low, mid, gates, out, x, y, z, load_sem, a2a_send, a2a_recv, raw_send, raw_recv, z_send, z_recv, out_sem):
    heights, gate = psi.shape[1], psi.shape[2]
    pairs = heights // 2
    part = gate // n_wide
    me = lax.axis_index("wide")
    mine = lax.axis_index("narrow")
    side = (mine // 2) % 2
    partner = mine + 2 - 4 * side

    barrier = pltpu.get_barrier_semaphore()

    def greet(d, _):
        pl.semaphore_signal(barrier, inc=1, device_id={"wide": lax.rem(me + d, n_wide)}, device_id_type=MESH)
        return 0

    pl.semaphore_signal(barrier, inc=1, device_id={"narrow": partner}, device_id_type=MESH)
    lax.fori_loop(1, n_wide, greet, 0)

    def load(h):
        return pltpu.make_async_copy(psi.at[:, h], x.at[h], load_sem.at[h])

    def start_load(h, _):
        load(h).start()
        return 0

    lax.fori_loop(0, heights, start_load, 0)
    pl.semaphore_wait(barrier, n_wide)

    def raw(j):
        return pltpu.make_async_remote_copy(
            src_ref=psi.at[:, j], dst_ref=x.at[heights + j], send_sem=raw_send.at[j], recv_sem=raw_recv.at[j],
            device_id={"narrow": partner}, device_id_type=MESH)

    def across(k):
        return pltpu.make_async_remote_copy(
            src_ref=y.at[pl.ds(2 * k, 2)], dst_ref=z.at[pl.ds(2 * k, 2)], send_sem=z_send.at[k], recv_sem=z_recv.at[k],
            device_id={"narrow": partner}, device_id_type=MESH)

    raw(0).start()
    raw(1).start()

    own_rows = pl.ds(pl.multiple_of(me * part, part), part)

    def scatter(slot, dst, dst_slot):
        def send(d, _):
            to = lax.rem(me + d, n_wide)
            pltpu.make_async_remote_copy(
                src_ref=x.at[slot, :, pl.ds(pl.multiple_of(to * part, part), part)],
                dst_ref=dst.at[dst_slot, :, own_rows],
                send_sem=a2a_send.at[slot], recv_sem=a2a_recv.at[slot],
                device_id={"wide": to}, device_id_type=MESH).start()
            return 0

        lax.fori_loop(1, n_wide, send, 0)
        dst[dst_slot, :, own_rows] = x[slot, :, own_rows]

    def all_but_own(ref, slot, sem):
        view = ref.at[slot, :, pl.ds(0, (n_wide - 1) * part)]
        pltpu.make_async_copy(view, view, sem).wait()

    def compute_pair(k):
        def one(h, _):
            load(h).wait()
            merged(x, h, low, mid)
            scatter(h, y, h)
            return 0

        lax.fori_loop(2 * k, 2 * k + 2, one, 0)

    def gathered(k):
        all_but_own(y, 2 * k, a2a_recv.at[2 * k])
        all_but_own(y, 2 * k + 1, a2a_recv.at[2 * k + 1])
        pair_on(y, (2 * k, 2 * k + 1), part, gates, 0)

    compute_pair(1)

    def pipeline(k, _):
        compute_pair(lax.rem(k + 1, pairs))
        gathered(k)
        across(k).start()
        return 0

    lax.fori_loop(1, pairs, pipeline, 0)
    gathered(0)

    def far_one(j, _):
        raw(j).wait_recv()
        merged(x, heights + j, low, mid)
        scatter(heights + j, z, j)
        return 0

    lax.fori_loop(0, 2, far_one, 0)
    all_but_own(z, 0, a2a_recv.at[heights])
    all_but_own(z, 1, a2a_recv.at[heights + 1])
    pair_on(z, (0, 1), part, gates, 0)
    combine(y, z, (0, 1), side, gates)

    def leave(h):
        return pltpu.make_async_copy(z.at[h], out.at[:, h], out_sem.at[h])

    def start_leave(h, _):
        leave(h).start()
        return 0

    def quad(hh, k):
        across(k).wait_recv()
        combine(y, z, (2 * k, 2 * k + 1), side, gates)
        pair_on(z, (4 * hh, 4 * hh + 2), 4 * part, gates, 1)
        pair_on(z, (4 * hh + 1, 4 * hh + 3), 4 * part, gates, 1)
        lax.fori_loop(4 * hh, 4 * hh + 4, start_leave, 0)

    quad(0, 1)

    def finish(hh, _):
        across(2 * hh).wait_recv()
        combine(y, z, (4 * hh, 4 * hh + 1), side, gates)
        quad(hh, 2 * hh + 1)
        return 0

    lax.fori_loop(1, heights // 4, finish, 0)

    def drain(h, _):
        leave(h).wait()
        return 0

    lax.fori_loop(0, heights, drain, 0)

    def sent(slot, _):
        all_but_own(x, slot, a2a_send.at[slot])
        return 0

    lax.fori_loop(0, heights + 2, sent, 0)

    def sent_across(k, _):
        across(k).wait_send()
        return 0

    lax.fori_loop(1, pairs, sent_across, 0)
    raw(0).wait_send()
    raw(1).wait_send()


def body(n_wide, amplitudes, low_gate, mid_gate, pair_gates):
    shape = amplitudes.shape
    psi = amplitudes.reshape(shape[0], shape[3], shape[4], shape[5])
    heights, gate, lanes = psi.shape[1:]
    dma = pltpu.SemaphoreType.DMA
    state = pl.pallas_call(
        functools.partial(kernel, n_wide),
        out_shape=jax.ShapeDtypeStruct(psi.shape, jnp.float32),
        in_specs=[
            pl.BlockSpec(memory_space=pl.ANY),
            pl.BlockSpec(memory_space=pltpu.VMEM),
            pl.BlockSpec(memory_space=pltpu.VMEM),
            pl.BlockSpec(memory_space=pltpu.SMEM),
        ],
        out_specs=pl.BlockSpec(memory_space=pl.ANY),
        scratch_shapes=[
            pltpu.VMEM((heights + 2, 2, gate, lanes), jnp.float32),
            pltpu.VMEM((heights, 2, gate, lanes), jnp.float32),
            pltpu.VMEM((heights, 2, gate, lanes), jnp.float32),
            dma((heights,)),
            dma((heights + 2,)),
            dma((heights + 2,)),
            dma((2,)),
            dma((2,)),
            dma((heights // 2,)),
            dma((heights // 2,)),
            dma((heights,)),
        ],
        compiler_params=pltpu.CompilerParams(
            collective_id=0, has_side_effects=True, vmem_limit_bytes=52 * 2**20
        ),
    )(psi, low_gate, mid_gate, pair_gates.reshape(-1))
    return state.reshape(shape)


def solution(mesh):
    in_specs = (P(None, "wide", "narrow", None, None, None), P(), P(), P())
    out_specs = P(None, "wide", "narrow", None, None, None)
    return jax.shard_map(
        functools.partial(body, mesh.shape["wide"]), mesh=mesh, in_specs=in_specs, out_specs=out_specs, check_vma=False
    )
```

time: 863 us -> 383 us (0.44); the launches traced: 853 us -> 383 us
  waiting for transfers between devices: 532 us -> 0 us
  Pallas kernels: 0 us -> 372 us
  other arithmetic: 104 us -> 0 us
  blocking collectives: 97.8 us -> 0 us
  local copies, waits for them, and re-layouts: 66.9 us -> 10.5 us
  matrix products: 45.5 us -> 0 us
    ppermute x3 -> x0, waiting for transfers between devices: 532 us -> none  [swapped(): lax.ppermute(x, axis, [(i, i ^ 1 << bit) for i in range(lax.axis_size(axi...]
    pallas_call x0 -> x1, Pallas kernels: none -> 372 us  [body(): pl.pallas_call(functools.partial(kernel, n_wide), out_shape=jax.ShapeDtyp...]
    all_to_all x1 -> x0, blocking collectives: 97.8 us -> none  [remap_qubits(): lax.all_to_all(state, 'wide', split_axis=4, concat_axis=4, tiled=True)]
    sub x6 -> x0, other arithmetic: 53.6 us -> none  [partner_gate(): total_real + coef_real * amplitude[0] - coef_imag * amplitude[1]]
    dot_general x8 -> x0, matrix products: 45.5 us -> none  [the longest x1 7.52 us: apply_merged(): jnp.einsum('abhml,im->abhil', first_imag, mid_imag, precision=highest)]
    add x4 -> x0, other arithmetic: 34.7 us -> none  [partner_gate(): total_imag + coef_real * amplitude[1] + coef_imag * amplitude[0]]
    slice x10 -> x0, local copies, waits for them, and re-layouts: 23.4 us -> none  [the longest x2 11.5 us: partner_gate(): amplitude[1]]
    unnamed x34 -> x5, local copies, waits for them, and re-layouts: 25.4 us -> 9.73 us
  transfers between devices with their start and end apart: 3 -> 0, of which waited for: 2 -> 0; matrix products, arithmetic and copies ran while one was open for 4% -> 0% of each run, Pallas kernels for 0% -> 0%
where the time goes in v1:
time: 383 us
  Pallas kernels  372 us (97%)
  local copies, waits for them, and re-layouts  10.5 us (3%)
    pallas_call x1, Pallas kernels, body(): pl.pallas_call(functools.partial(kernel, n_wide), out_shape=jax.ShapeDtyp...  372 us
    unnamed x5, local copies, waits for them, and re-layouts  9.73 us

profile of v1, /device:TPU:0, one launch (start us, length us, event | category | flops | bytes accessed | tf_op | source)
XLA Modules:
  0.0 382.9 jit_solution(12119983662964002918)
XLA Ops:
  0.0 0.8 reshape.10.gates
  0.8 0.0 copy-start
  0.8 1.0 copy-done
  1.9 0.0 copy-start.1
  1.9 1.0 copy-done.1
  2.9 372.4 %shard_map.46 = f32[2,16,256,256]{3,2,1,0:T(8,128)} custom-call(f32[2,16,256,256]{3,2,1,0:T(8,128)} %bitcast.5, f32[2,256,256]{2,1,0:T(8,128)S(1)} %copy-done, f32[2,256,256]{2,1,0:T(8,128)S(1)} %copy-done.1, f32[96]{0:T(128)S(1)} %reshape.10.gates), custom_call_target="tpu_custom_call" | custom-call | tf_op jit(solution)/shard_map/pallas_call | solution.py:227
  375.3 7.7 %copy.7 = f32[2,1,1,16,256,256]{5,4,3,2,1,0:T(8,128)} copy(f32[2,1,1,16,256,256]{5,4,3,2,1,0:T(8,128)} %bitcast.4) | data formatting | bytes 16777216
Async XLA Ops:
  0.8 1.0 copy-start
  1.9 1.0 copy-start.1

commit v2 on v1

--- a/solution.py
+++ b/solution.py
@@ -37,36 +37,35 @@
     return real, imag
 
 
-def pair_on(ref, slots, stride, gates, which):
+def pair_on(ref, into, slots, stride, gates, which, low_row, span):
     coefs = [
-        [(gates[which * 32 + row * 4 + col], gates[which * 32 + 16 + row * 4 + col]) for col in range(4)]
+        [(gates[which, 0, row, col], gates[which, 1, row, col]) for col in range(4)]
         for row in range(4)
     ]
-    per = stride // CHUNK
+    per = span // CHUNK
 
     def step(i, _):
-        base = pl.multiple_of((i // per) * (2 * stride) + (i % per) * CHUNK, CHUNK)
+        base = pl.multiple_of((i // per) * (2 * stride) + low_row + (i % per) * CHUNK, CHUNK)
         far = pl.multiple_of(base + stride, CHUNK)
         places = [(slots[b], pl.ds(start, CHUNK)) for start in (base, far) for b in range(2)]
         sources = [(ref[s, 0, rows], ref[s, 1, rows]) for s, rows in places]
         results = [mix(coefs[row], sources) for row in range(4)]
         for (s, rows), (real, imag) in zip(places, results):
-            ref[s, 0, rows] = real
-            ref[s, 1, rows] = imag
-        return 0
-
-    lax.fori_loop(0, ref.shape[2] // (2 * CHUNK), step, 0)
-
-
-def combine(own, far, slots, side, gates):
+            into(s, rows, real, imag)
+        return 0
+
+    lax.fori_loop(0, ref.shape[2] // (2 * stride) * per, step, 0)
+
+
+def combine(own, far, slots, side, gates, block, low_row, span):
     def coef(q, a, b):
-        at = 64 + (2 * side + q) * 4 + 2 * a + b
-        return gates[at], gates[at + 16]
+        return gates[2, 0, 2 * side + q, 2 * a + b], gates[2, 1, 2 * side + q, 2 * a + b]
 
     coefs = [[coef(q, side, 0), coef(q, side, 1), coef(q, 1 - side, 0), coef(q, 1 - side, 1)] for q in range(2)]
+    per = span // CHUNK
 
     def step(i, _):
-        rows = pl.ds(pl.multiple_of(i * CHUNK, CHUNK), CHUNK)
+        rows = pl.ds(pl.multiple_of((i // per) * block + low_row + (i % per) * CHUNK, CHUNK), CHUNK)
         sources = [(ref[s, 0, rows], ref[s, 1, rows]) for ref in (own, far) for s in slots]
         results = [mix(coefs[q], sources) for q in range(2)]
         for s, (real, imag) in zip(slots, results):
@@ -74,13 +73,15 @@
             far[s, 1, rows] = imag
         return 0
 
-    lax.fori_loop(0, far.shape[2] // CHUNK, step, 0)
-
-
-def kernel(n_wide, psi, low, mid, gates, out, x, y, z, load_sem, a2a_send, a2a_recv, raw_send, raw_recv, z_send, z_recv, out_sem):
+    lax.fori_loop(0, far.shape[2] // block * per, step, 0)
+
+
+def kernel(n_wide, psi, low_hbm, mid_hbm, gates, out, x, y, z, low, mid, load_sem, gate_sem, a2a_send, a2a_recv, raw_send, raw_recv, z_send, z_recv):
     heights, gate = psi.shape[1], psi.shape[2]
     pairs = heights // 2
     part = gate // n_wide
+    block = 4 * part
+    last = pairs - 1
     me = lax.axis_index("wide")
     mine = lax.axis_index("narrow")
     side = (mine // 2) % 2
@@ -102,7 +103,8 @@
         load(h).start()
         return 0
 
-    lax.fori_loop(0, heights, start_load, 0)
+    fetch_low = pltpu.make_async_copy(low_hbm, low, gate_sem.at[0])
+    fetch_mid = pltpu.make_async_copy(mid_hbm, mid, gate_sem.at[1])
     pl.semaphore_wait(barrier, n_wide)
 
     def raw(j):
@@ -115,8 +117,24 @@
             src_ref=y.at[pl.ds(2 * k, 2)], dst_ref=z.at[pl.ds(2 * k, 2)], send_sem=z_send.at[k], recv_sem=z_recv.at[k],
             device_id={"narrow": partner}, device_id_type=MESH)
 
+    def start_piece(j):
+        for at in range(j * part, gate, block):
+            rows = pl.ds(at, part)
+            pltpu.make_async_remote_copy(
+                src_ref=y.at[pl.ds(2 * last, 2), :, rows], dst_ref=z.at[pl.ds(2 * last, 2), :, rows],
+                send_sem=z_send.at[last + j], recv_sem=z_recv.at[last + j],
+                device_id={"narrow": partner}, device_id_type=MESH).start()
+
+    def wait_piece(ref, sem):
+        view = ref.at[pl.ds(2 * last, 2), :, pl.ds(0, gate // 4)]
+        pltpu.make_async_copy(view, view, sem).wait()
+
     raw(0).start()
     raw(1).start()
+    fetch_low.start()
+    fetch_mid.start()
+    lax.fori_loop(2, heights, start_load, 0)
+    lax.fori_loop(0, 2, start_load, 0)
 
     own_rows = pl.ds(pl.multiple_of(me * part, part), part)
 
@@ -146,17 +164,34 @@
 
         lax.fori_loop(2 * k, 2 * k + 2, one, 0)
 
+    def in_place(ref):
+        def into(s, rows, real, imag):
+            ref[s, 0, rows] = real
+            ref[s, 1, rows] = imag
+
+        return into
+
+    def leave(s, rows, real, imag):
+        out[0, s, rows] = real
+        out[1, s, rows] = imag
+
     def gathered(k):
         all_but_own(y, 2 * k, a2a_recv.at[2 * k])
         all_but_own(y, 2 * k + 1, a2a_recv.at[2 * k + 1])
-        pair_on(y, (2 * k, 2 * k + 1), part, gates, 0)
-
+        pair_on(y, in_place(y), (2 * k, 2 * k + 1), part, gates, 0, 0, part)
+
+    fetch_low.wait()
+    fetch_mid.wait()
     compute_pair(1)
 
     def pipeline(k, _):
         compute_pair(lax.rem(k + 1, pairs))
         gathered(k)
-        across(k).start()
+
+        @pl.when(k <= 2)
+        def _():
+            across(k).start()
+
         return 0
 
     lax.fori_loop(1, pairs, pipeline, 0)
@@ -171,38 +206,45 @@
     lax.fori_loop(0, 2, far_one, 0)
     all_but_own(z, 0, a2a_recv.at[heights])
     all_but_own(z, 1, a2a_recv.at[heights + 1])
-    pair_on(z, (0, 1), part, gates, 0)
-    combine(y, z, (0, 1), side, gates)
-
-    def leave(h):
-        return pltpu.make_async_copy(z.at[h], out.at[:, h], out_sem.at[h])
-
-    def start_leave(h, _):
-        leave(h).start()
-        return 0
+    pair_on(z, in_place(z), (0, 1), part, gates, 0, 0, part)
+    combine(y, z, (0, 1), side, gates, block, 0, block)
+
+    def arrived(k):
+        across(k).wait_recv()
+
+        @pl.when(k + 2 < last)
+        def _():
+            across(k + 2).start()
+
+    def close(hh, low_row, span):
+        for b in range(2):
+            pair_on(z, leave, (4 * hh + b, 4 * hh + 2 + b), block, gates, 1, low_row, span)
 
     def quad(hh, k):
-        across(k).wait_recv()
-        combine(y, z, (2 * k, 2 * k + 1), side, gates)
-        pair_on(z, (4 * hh, 4 * hh + 2), 4 * part, gates, 1)
-        pair_on(z, (4 * hh + 1, 4 * hh + 3), 4 * part, gates, 1)
-        lax.fori_loop(4 * hh, 4 * hh + 4, start_leave, 0)
+        arrived(k)
+        combine(y, z, (2 * k, 2 * k + 1), side, gates, block, 0, block)
+        close(hh, 0, block)
 
     quad(0, 1)
+    quads = heights // 4
 
     def finish(hh, _):
-        across(2 * hh).wait_recv()
-        combine(y, z, (4 * hh, 4 * hh + 1), side, gates)
+        arrived(2 * hh)
+        combine(y, z, (4 * hh, 4 * hh + 1), side, gates, block, 0, block)
         quad(hh, 2 * hh + 1)
         return 0
 
-    lax.fori_loop(1, heights // 4, finish, 0)
-
-    def drain(h, _):
-        leave(h).wait()
-        return 0
-
-    lax.fori_loop(0, heights, drain, 0)
+    lax.fori_loop(1, quads - 1, finish, 0)
+    start_piece(0)
+    across(last - 1).wait_recv()
+    start_piece(1)
+    combine(y, z, (2 * last - 2, 2 * last - 1), side, gates, block, 0, block)
+    for j in range(4):
+        wait_piece(z, z_recv.at[last + j])
+        if j < 2:
+            start_piece(j + 2)
+        combine(y, z, (2 * last, 2 * last + 1), side, gates, block, j * part, part)
+        close(quads - 1, j * part, part)
 
     def sent(slot, _):
         all_but_own(x, slot, a2a_send.at[slot])
@@ -214,7 +256,9 @@
         across(k).wait_send()
         return 0
 
-    lax.fori_loop(1, pairs, sent_across, 0)
+    lax.fori_loop(1, last, sent_across, 0)
+    for j in range(4):
+        wait_piece(y, z_send.at[last + j])
     raw(0).wait_send()
     raw(1).wait_send()
 
@@ -228,29 +272,31 @@
         functools.partial(kernel, n_wide),
         out_shape=jax.ShapeDtypeStruct(psi.shape, jnp.float32),
         in_specs=[
-            pl.BlockSpec(memory_space=pl.ANY),
-            pl.BlockSpec(memory_space=pltpu.VMEM),
-            pl.BlockSpec(memory_space=pltpu.VMEM),
+            pl.BlockSpec(memory_space=pltpu.HBM),
+            pl.BlockSpec(memory_space=pltpu.HBM),
+            pl.BlockSpec(memory_space=pltpu.HBM),
             pl.BlockSpec(memory_space=pltpu.SMEM),
         ],
-        out_specs=pl.BlockSpec(memory_space=pl.ANY),
+        out_specs=pl.BlockSpec(memory_space=pltpu.VMEM),
         scratch_shapes=[
             pltpu.VMEM((heights + 2, 2, gate, lanes), jnp.float32),
             pltpu.VMEM((heights, 2, gate, lanes), jnp.float32),
             pltpu.VMEM((heights, 2, gate, lanes), jnp.float32),
+            pltpu.VMEM(low_gate.shape, jnp.float32),
+            pltpu.VMEM(mid_gate.shape, jnp.float32),
             dma((heights,)),
+            dma((2,)),
             dma((heights + 2,)),
             dma((heights + 2,)),
             dma((2,)),
             dma((2,)),
-            dma((heights // 2,)),
-            dma((heights // 2,)),
-            dma((heights,)),
+            dma((heights // 2 + 3,)),
+            dma((heights // 2 + 3,)),
         ],
         compiler_params=pltpu.CompilerParams(
-            collective_id=0, has_side_effects=True, vmem_limit_bytes=52 * 2**20
+            collective_id=0, has_side_effects=True, vmem_limit_bytes=40 * 2**20
         ),
-    )(psi, low_gate, mid_gate, pair_gates.reshape(-1))
+    )(psi, low_gate, mid_gate, pair_gates)
     return state.reshape(shape)
 
 

time: 383 us -> 376 us (0.982)
  local copies, waits for them, and re-layouts: 10.5 us -> 6.19 us
    unnamed x5 -> x7, local copies, waits for them, and re-layouts: 9.73 us -> 6.19 us
where the time goes in v2:
time: 376 us
  Pallas kernels  370 us (98%)
  local copies, waits for them, and re-layouts  6.19 us (2%)
    pallas_call x1, Pallas kernels, body(): pl.pallas_call(functools.partial(kernel, n_wide), out_shape=jax.ShapeDtyp...  370 us

profile of v2, /device:TPU:0, one launch (start us, length us, event | category | flops | bytes accessed | tf_op | source)
XLA Modules:
  0.0 375.7 jit_solution(9267171093880258094)
XLA Ops:
  0.0 0.0 copy-start
  0.0 1.0 copy-done
  1.0 0.0 copy-start.1
  1.0 1.0 copy-done.1
  2.1 0.0 copy-start.2
  2.1 0.7 copy-done.2
  2.8 369.5 %shard_map.46 = f32[2,16,256,256]{3,2,1,0:T(8,128)S(1)} custom-call(f32[2,16,256,256]{3,2,1,0:T(8,128)} %bitcast.5, f32[2,256,256]{2,1,0:T(8,128)S(1)} %copy-done, f32[2,256,256]{2,1,0:T(8,128)S(1)} %copy-done.1, f32[3,2,4,4]{3,2,1,0:T(4,128)S(1)} %copy-done.2), custom_call_target="tpu_custom_call" | custom-call | tf_op jit(solution)/shard_map/pallas_call | solution.py:271
  372.3 3.4 copy.7
Async XLA Ops:
  0.0 1.0 copy-start
  1.0 1.0 copy-start.1
  2.1 0.7 copy-start.2

commit v3 on v2

--- a/solution.py
+++ b/solution.py
@@ -76,7 +76,7 @@
     lax.fori_loop(0, far.shape[2] // block * per, step, 0)
 
 
-def kernel(n_wide, psi, low_hbm, mid_hbm, gates, out, x, y, z, low, mid, load_sem, gate_sem, a2a_send, a2a_recv, raw_send, raw_recv, z_send, z_recv):
+def kernel(n_wide, psi, low_hbm, mid_hbm, gates_hbm, out, x, y, z, low, mid, gates, load_sem, gate_sem, a2a_send, a2a_recv, raw_send, raw_recv, z_send, z_recv):
     heights, gate = psi.shape[1], psi.shape[2]
     pairs = heights // 2
     part = gate // n_wide
@@ -105,6 +105,7 @@
 
     fetch_low = pltpu.make_async_copy(low_hbm, low, gate_sem.at[0])
     fetch_mid = pltpu.make_async_copy(mid_hbm, mid, gate_sem.at[1])
+    fetch_gates = pltpu.make_async_copy(gates_hbm, gates, gate_sem.at[2])
     pl.semaphore_wait(barrier, n_wide)
 
     def raw(j):
@@ -133,6 +134,7 @@
     raw(1).start()
     fetch_low.start()
     fetch_mid.start()
+    fetch_gates.start()
     lax.fori_loop(2, heights, start_load, 0)
     lax.fori_loop(0, 2, start_load, 0)
 
@@ -183,12 +185,13 @@
     fetch_low.wait()
     fetch_mid.wait()
     compute_pair(1)
+    fetch_gates.wait()
 
     def pipeline(k, _):
         compute_pair(lax.rem(k + 1, pairs))
         gathered(k)
 
-        @pl.when(k <= 2)
+        @pl.when(k <= 3)
         def _():
             across(k).start()
 
@@ -212,7 +215,7 @@
     def arrived(k):
         across(k).wait_recv()
 
-        @pl.when(k + 2 < last)
+        @pl.when(jnp.logical_and(k + 2 > 3, k + 2 < last))
         def _():
             across(k + 2).start()
 
@@ -275,7 +278,7 @@
             pl.BlockSpec(memory_space=pltpu.HBM),
             pl.BlockSpec(memory_space=pltpu.HBM),
             pl.BlockSpec(memory_space=pltpu.HBM),
-            pl.BlockSpec(memory_space=pltpu.SMEM),
+            pl.BlockSpec(memory_space=pltpu.HBM),
         ],
         out_specs=pl.BlockSpec(memory_space=pltpu.VMEM),
         scratch_shapes=[
@@ -284,8 +287,9 @@
             pltpu.VMEM((heights, 2, gate, lanes), jnp.float32),
             pltpu.VMEM(low_gate.shape, jnp.float32),
             pltpu.VMEM(mid_gate.shape, jnp.float32),
+            pltpu.SMEM(pair_gates.shape, jnp.float32),
             dma((heights,)),
-            dma((2,)),
+            dma((3,)),
             dma((heights + 2,)),
             dma((heights + 2,)),
             dma((2,)),
@@ -296,7 +300,7 @@
         compiler_params=pltpu.CompilerParams(
             collective_id=0, has_side_effects=True, vmem_limit_bytes=40 * 2**20
         ),
-    )(psi, low_gate, mid_gate, pair_gates)
+    )(*[pltpu.with_memory_space_constraint(array, pltpu.HBM) for array in (psi, low_gate, mid_gate, pair_gates)])
     return state.reshape(shape)
 
 

time: 376 us -> 372 us (0.989)
  no operation moved by 1% of the time
where the time goes in v3:
time: 372 us
  Pallas kernels  369 us (99%)
    pallas_call x1, Pallas kernels, body(): pl.pallas_call(functools.partial(kernel, n_wide), out_shape=jax.ShapeDtyp...  369 us

profile of v3, /device:TPU:0, one launch (start us, length us, event | category | flops | bytes accessed | tf_op | source)
XLA Modules:
  0.0 372.2 jit_solution(12410087214152617959)
XLA Ops:
  0.0 368.8 %shard_map.46 = f32[2,16,256,256]{3,2,1,0:T(8,128)S(1)} custom-call(f32[2,16,256,256]{3,2,1,0:T(8,128)} %bitcast.5, f32[2,256,256]{2,1,0:T(8,128)} %low_hbm.1, f32[2,256,256]{2,1,0:T(8,128)} %mid_hbm.1, f32[3,2,4,4]{3,2,1,0:T(4,128)} %gates_hbm.1), custom_call_target="tpu_custom_call" | custom-call | tf_op jit(solution)/shard_map/pallas_call | solution.py:274
  368.8 3.4 copy.7

commit v4 on v3

--- a/solution.py
+++ b/solution.py
@@ -9,6 +9,7 @@
 
 MESH = pl.DeviceIdType.MESH
 CHUNK = 8
+PIECES = 8
 highest = lax.Precision.HIGHEST
 
 
@@ -76,16 +77,19 @@
     lax.fori_loop(0, far.shape[2] // block * per, step, 0)
 
 
-def kernel(n_wide, psi, low_hbm, mid_hbm, gates_hbm, out, x, y, z, low, mid, gates, load_sem, gate_sem, a2a_send, a2a_recv, raw_send, raw_recv, z_send, z_recv):
+def kernel(n_wide, n_narrow, psi, low_hbm, mid_hbm, gates_hbm, out, x, y, z, low, mid, gates, load_sem, gate_sem, a2a_send, a2a_recv, raw_send, raw_recv, z_send, z_recv):
     heights, gate = psi.shape[1], psi.shape[2]
     pairs = heights // 2
     part = gate // n_wide
     block = 4 * part
     last = pairs - 1
+    span = block // PIECES
     me = lax.axis_index("wide")
     mine = lax.axis_index("narrow")
     side = (mine // 2) % 2
     partner = mine + 2 - 4 * side
+    outer = jnp.logical_or(mine == 0, mine == n_narrow - 1)
+    inner = jnp.logical_not(outer)
 
     barrier = pltpu.get_barrier_semaphore()
 
@@ -119,15 +123,15 @@
             device_id={"narrow": partner}, device_id_type=MESH)
 
     def start_piece(j):
-        for at in range(j * part, gate, block):
-            rows = pl.ds(at, part)
+        for at in range(j * span, gate, block):
+            rows = pl.ds(at, span)
             pltpu.make_async_remote_copy(
                 src_ref=y.at[pl.ds(2 * last, 2), :, rows], dst_ref=z.at[pl.ds(2 * last, 2), :, rows],
                 send_sem=z_send.at[last + j], recv_sem=z_recv.at[last + j],
                 device_id={"narrow": partner}, device_id_type=MESH).start()
 
     def wait_piece(ref, sem):
-        view = ref.at[pl.ds(2 * last, 2), :, pl.ds(0, gate // 4)]
+        view = ref.at[pl.ds(2 * last, 2), :, pl.ds(0, gate // PIECES)]
         pltpu.make_async_copy(view, view, sem).wait()
 
     raw(0).start()
@@ -239,15 +243,10 @@
 
     lax.fori_loop(1, quads - 1, finish, 0)
     start_piece(0)
-    across(last - 1).wait_recv()
-    start_piece(1)
-    combine(y, z, (2 * last - 2, 2 * last - 1), side, gates, block, 0, block)
-    for j in range(4):
-        wait_piece(z, z_recv.at[last + j])
-        if j < 2:
-            start_piece(j + 2)
-        combine(y, z, (2 * last, 2 * last + 1), side, gates, block, j * part, part)
-        close(quads - 1, j * part, part)
+
+    @pl.when(inner)
+    def _():
+        start_piece(1)
 
     def sent(slot, _):
         all_but_own(x, slot, a2a_send.at[slot])
@@ -259,20 +258,49 @@
         across(k).wait_send()
         return 0
 
-    lax.fori_loop(1, last, sent_across, 0)
-    for j in range(4):
-        wait_piece(y, z_send.at[last + j])
     raw(0).wait_send()
     raw(1).wait_send()
-
-
-def body(n_wide, amplitudes, low_gate, mid_gate, pair_gates):
+    across(last - 1).wait_recv()
+    combine(y, z, (2 * last - 2, 2 * last - 1), side, gates, block, 0, block)
+    for j in range(PIECES):
+        wait_piece(z, z_recv.at[last + j])
+        if j + 1 < PIECES:
+            @pl.when(outer)
+            def _():
+                start_piece(j + 1)
+
+        if j + 2 < PIECES:
+            @pl.when(inner)
+            def _():
+                start_piece(j + 2)
+
+        if j == PIECES - 2:
+            lax.fori_loop(1, last, sent_across, 0)
+        combine(y, z, (2 * last, 2 * last + 1), side, gates, block, j * span, span)
+        close(quads - 1, j * span, span)
+
+    for j in range(PIECES):
+        wait_piece(y, z_send.at[last + j])
+
+
+def write(state, out, sems):
+    copies = [
+        pltpu.make_async_copy(state.at[c, h], out.at[c, h], sems.at[c, h])
+        for c in range(state.shape[0]) for h in range(state.shape[1])
+    ]
+    for copy in copies:
+        copy.start()
+    for copy in copies:
+        copy.wait()
+
+
+def body(n_wide, n_narrow, amplitudes, low_gate, mid_gate, pair_gates):
     shape = amplitudes.shape
     psi = amplitudes.reshape(shape[0], shape[3], shape[4], shape[5])
     heights, gate, lanes = psi.shape[1:]
     dma = pltpu.SemaphoreType.DMA
     state = pl.pallas_call(
-        functools.partial(kernel, n_wide),
+        functools.partial(kernel, n_wide, n_narrow),
         out_shape=jax.ShapeDtypeStruct(psi.shape, jnp.float32),
         in_specs=[
             pl.BlockSpec(memory_space=pltpu.HBM),
@@ -294,19 +322,27 @@
             dma((heights + 2,)),
             dma((2,)),
             dma((2,)),
-            dma((heights // 2 + 3,)),
-            dma((heights // 2 + 3,)),
+            dma((heights // 2 - 1 + PIECES,)),
+            dma((heights // 2 - 1 + PIECES,)),
         ],
         compiler_params=pltpu.CompilerParams(
             collective_id=0, has_side_effects=True, vmem_limit_bytes=40 * 2**20
         ),
     )(*[pltpu.with_memory_space_constraint(array, pltpu.HBM) for array in (psi, low_gate, mid_gate, pair_gates)])
-    return state.reshape(shape)
+    result = pl.pallas_call(
+        write,
+        out_shape=jax.ShapeDtypeStruct(psi.shape, jnp.float32),
+        in_specs=[pl.BlockSpec(memory_space=pltpu.VMEM)],
+        out_specs=pl.BlockSpec(memory_space=pltpu.HBM),
+        scratch_shapes=[dma(psi.shape[:2])],
+        compiler_params=pltpu.CompilerParams(vmem_limit_bytes=16 * 2**20),
+    )(state)
+    return result.reshape(shape)
 
 
 def solution(mesh):
     in_specs = (P(None, "wide", "narrow", None, None, None), P(), P(), P())
     out_specs = P(None, "wide", "narrow", None, None, None)
     return jax.shard_map(
-        functools.partial(body, mesh.shape["wide"]), mesh=mesh, in_specs=in_specs, out_specs=out_specs, check_vma=False
+        functools.partial(body, mesh.shape["wide"], mesh.shape["narrow"]), mesh=mesh, in_specs=in_specs, out_specs=out_specs, check_vma=False
     )

time: 372 us -> 373 us (level)
  Pallas kernels: 369 us -> 373 us
    pallas_call x1 -> x2, Pallas kernels: 369 us -> 373 us  [the longest x1 369 us: body(): pl.pallas_call(functools.partial(kernel, n_wide, n_narrow), out_shape=jax...]
where the time goes in v4:
time: 373 us
  Pallas kernels  373 us (100%)
    pallas_call x1, Pallas kernels, body(): pl.pallas_call(functools.partial(kernel, n_wide, n_narrow), out_shape=jax...  369 us

profile of v4, /device:TPU:0, one launch (start us, length us, event | category | flops | bytes accessed | tf_op | source)
XLA Modules:
  0.0 372.8 jit_solution(8597609367782934782)
XLA Ops:
  0.0 369.3 %shard_map.46.state = f32[2,16,256,256]{3,2,1,0:T(8,128)S(1)} custom-call(f32[2,16,256,256]{3,2,1,0:T(8,128)} %bitcast.4, f32[2,256,256]{2,1,0:T(8,128)} %low_hbm.1, f32[2,256,256]{2,1,0:T(8,128)} %mid_hbm.1, f32[3,2,4,4]{3,2,1,0:T(4,128)} %gates_hbm.1), custom_call_target="tpu_custom_call" | custom-call | tf_op jit(solution)/shard_map/pallas_call | solution.py:302
  369.3 3.5 shard_map.47

commit v5 on v3

--- a/solution.py
+++ b/solution.py
@@ -9,6 +9,8 @@
 
 MESH = pl.DeviceIdType.MESH
 CHUNK = 8
+PIECES = 8
+AHEAD = 4
 highest = lax.Precision.HIGHEST
 
 
@@ -82,6 +84,7 @@
     part = gate // n_wide
     block = 4 * part
     last = pairs - 1
+    span = block // PIECES
     me = lax.axis_index("wide")
     mine = lax.axis_index("narrow")
     side = (mine // 2) % 2
@@ -119,15 +122,15 @@
             device_id={"narrow": partner}, device_id_type=MESH)
 
     def start_piece(j):
-        for at in range(j * part, gate, block):
-            rows = pl.ds(at, part)
+        for at in range(j * span, gate, block):
+            rows = pl.ds(at, span)
             pltpu.make_async_remote_copy(
                 src_ref=y.at[pl.ds(2 * last, 2), :, rows], dst_ref=z.at[pl.ds(2 * last, 2), :, rows],
                 send_sem=z_send.at[last + j], recv_sem=z_recv.at[last + j],
                 device_id={"narrow": partner}, device_id_type=MESH).start()
 
     def wait_piece(ref, sem):
-        view = ref.at[pl.ds(2 * last, 2), :, pl.ds(0, gate // 4)]
+        view = ref.at[pl.ds(2 * last, 2), :, pl.ds(0, gate // PIECES)]
         pltpu.make_async_copy(view, view, sem).wait()
 
     raw(0).start()
@@ -238,16 +241,8 @@
         return 0
 
     lax.fori_loop(1, quads - 1, finish, 0)
-    start_piece(0)
-    across(last - 1).wait_recv()
-    start_piece(1)
-    combine(y, z, (2 * last - 2, 2 * last - 1), side, gates, block, 0, block)
-    for j in range(4):
-        wait_piece(z, z_recv.at[last + j])
-        if j < 2:
-            start_piece(j + 2)
-        combine(y, z, (2 * last, 2 * last + 1), side, gates, block, j * part, part)
-        close(quads - 1, j * part, part)
+    for j in range(AHEAD):
+        start_piece(j)
 
     def sent(slot, _):
         all_but_own(x, slot, a2a_send.at[slot])
@@ -259,11 +254,21 @@
         across(k).wait_send()
         return 0
 
-    lax.fori_loop(1, last, sent_across, 0)
-    for j in range(4):
-        wait_piece(y, z_send.at[last + j])
     raw(0).wait_send()
     raw(1).wait_send()
+    across(last - 1).wait_recv()
+    combine(y, z, (2 * last - 2, 2 * last - 1), side, gates, block, 0, block)
+    for j in range(PIECES):
+        wait_piece(z, z_recv.at[last + j])
+        if j + AHEAD < PIECES:
+            start_piece(j + AHEAD)
+        if j == PIECES - 2:
+            lax.fori_loop(1, last, sent_across, 0)
+        combine(y, z, (2 * last, 2 * last + 1), side, gates, block, j * span, span)
+        close(quads - 1, j * span, span)
+
+    for j in range(PIECES):
+        wait_piece(y, z_send.at[last + j])
 
 
 def body(n_wide, amplitudes, low_gate, mid_gate, pair_gates):
@@ -294,8 +299,8 @@
             dma((heights + 2,)),
             dma((2,)),
             dma((2,)),
-            dma((heights // 2 + 3,)),
-            dma((heights // 2 + 3,)),
+            dma((heights // 2 - 1 + PIECES,)),
+            dma((heights // 2 - 1 + PIECES,)),
         ],
         compiler_params=pltpu.CompilerParams(
             collective_id=0, has_side_effects=True, vmem_limit_bytes=40 * 2**20

time: 372 us -> 372 us (level)
  no operation moved by 1% of the time
where the time goes in v5:
time: 372 us
  Pallas kernels  368 us (99%)
    pallas_call x1, Pallas kernels, body(): pl.pallas_call(functools.partial(kernel, n_wide), out_shape=jax.ShapeDtyp...  368 us

profile of v5, /device:TPU:0, one launch (start us, length us, event | category | flops | bytes accessed | tf_op | source)
XLA Modules:
  0.0 371.8 jit_solution(4438378219199432230)
XLA Ops:
  0.0 368.3 %shard_map.46 = f32[2,16,256,256]{3,2,1,0:T(8,128)S(1)} custom-call(f32[2,16,256,256]{3,2,1,0:T(8,128)} %bitcast.5, f32[2,256,256]{2,1,0:T(8,128)} %low_hbm.1, f32[2,256,256]{2,1,0:T(8,128)} %mid_hbm.1, f32[3,2,4,4]{3,2,1,0:T(4,128)} %gates_hbm.1), custom_call_target="tpu_custom_call" | custom-call | tf_op jit(solution)/shard_map/pallas_call | solution.py:279
  368.4 3.4 copy.7

commit v6 on v5

--- a/solution.py
+++ b/solution.py
@@ -10,7 +10,8 @@
 MESH = pl.DeviceIdType.MESH
 CHUNK = 8
 PIECES = 8
-AHEAD = 4
+OUTER_AHEAD = 3
+INNER_AHEAD = 5
 highest = lax.Precision.HIGHEST
 
 
@@ -78,7 +79,7 @@
     lax.fori_loop(0, far.shape[2] // block * per, step, 0)
 
 
-def kernel(n_wide, psi, low_hbm, mid_hbm, gates_hbm, out, x, y, z, low, mid, gates, load_sem, gate_sem, a2a_send, a2a_recv, raw_send, raw_recv, z_send, z_recv):
+def kernel(n_wide, n_narrow, psi, low_hbm, mid_hbm, gates_hbm, out, x, y, z, low, mid, gates, load_sem, gate_sem, a2a_send, a2a_recv, raw_send, raw_recv, z_send, z_recv):
     heights, gate = psi.shape[1], psi.shape[2]
     pairs = heights // 2
     part = gate // n_wide
@@ -89,6 +90,8 @@
     mine = lax.axis_index("narrow")
     side = (mine // 2) % 2
     partner = mine + 2 - 4 * side
+    outer = jnp.logical_or(mine == 0, mine == n_narrow - 1)
+    inner = jnp.logical_not(outer)
 
     barrier = pltpu.get_barrier_semaphore()
 
@@ -241,8 +244,11 @@
         return 0
 
     lax.fori_loop(1, quads - 1, finish, 0)
-    for j in range(AHEAD):
-        start_piece(j)
+    for j in range(INNER_AHEAD):
+        if j < OUTER_AHEAD:
+            start_piece(j)
+        else:
+            pl.when(inner)(functools.partial(start_piece, j))
 
     def sent(slot, _):
         all_but_own(x, slot, a2a_send.at[slot])
@@ -260,8 +266,10 @@
     combine(y, z, (2 * last - 2, 2 * last - 1), side, gates, block, 0, block)
     for j in range(PIECES):
         wait_piece(z, z_recv.at[last + j])
-        if j + AHEAD < PIECES:
-            start_piece(j + AHEAD)
+        if j + OUTER_AHEAD < PIECES:
+            pl.when(outer)(functools.partial(start_piece, j + OUTER_AHEAD))
+        if j + INNER_AHEAD < PIECES:
+            pl.when(inner)(functools.partial(start_piece, j + INNER_AHEAD))
         if j == PIECES - 2:
             lax.fori_loop(1, last, sent_across, 0)
         combine(y, z, (2 * last, 2 * last + 1), side, gates, block, j * span, span)
@@ -271,13 +279,13 @@
         wait_piece(y, z_send.at[last + j])
 
 
-def body(n_wide, amplitudes, low_gate, mid_gate, pair_gates):
+def body(n_wide, n_narrow, amplitudes, low_gate, mid_gate, pair_gates):
     shape = amplitudes.shape
     psi = amplitudes.reshape(shape[0], shape[3], shape[4], shape[5])
     heights, gate, lanes = psi.shape[1:]
     dma = pltpu.SemaphoreType.DMA
     state = pl.pallas_call(
-        functools.partial(kernel, n_wide),
+        functools.partial(kernel, n_wide, n_narrow),
         out_shape=jax.ShapeDtypeStruct(psi.shape, jnp.float32),
         in_specs=[
             pl.BlockSpec(memory_space=pltpu.HBM),
@@ -313,5 +321,5 @@
     in_specs = (P(None, "wide", "narrow", None, None, None), P(), P(), P())
     out_specs = P(None, "wide", "narrow", None, None, None)
     return jax.shard_map(
-        functools.partial(body, mesh.shape["wide"]), mesh=mesh, in_specs=in_specs, out_specs=out_specs, check_vma=False
+        functools.partial(body, mesh.shape["wide"], mesh.shape["narrow"]), mesh=mesh, in_specs=in_specs, out_specs=out_specs, check_vma=False
     )

time: 372 us -> 372 us (level)
  no operation moved by 1% of the time
where the time goes in v6:
time: 372 us
  Pallas kernels  368 us (99%)
    pallas_call x1, Pallas kernels, body(): pl.pallas_call(functools.partial(kernel, n_wide, n_narrow), out_shape=jax...  368 us

profile of v6, /device:TPU:0, one launch (start us, length us, event | category | flops | bytes accessed | tf_op | source)
XLA Modules:
  0.0 371.8 jit_solution(18394325096018073433)
XLA Ops:
  0.0 368.3 %shard_map.46 = f32[2,16,256,256]{3,2,1,0:T(8,128)S(1)} custom-call(f32[2,16,256,256]{3,2,1,0:T(8,128)} %bitcast.5, f32[2,256,256]{2,1,0:T(8,128)} %low_hbm.1, f32[2,256,256]{2,1,0:T(8,128)} %mid_hbm.1, f32[3,2,4,4]{3,2,1,0:T(4,128)} %gates_hbm.1), custom_call_target="tpu_custom_call" | custom-call | tf_op jit(solution)/shard_map/pallas_call | solution.py:287
  368.4 3.4 copy.7
